TPU v7x, 256 devices: a whole 4x4x8 slice. The times are simulated.
256 devices in a mesh: ctx: 32 (over z, y_lo, core), tp: 8 (over y_hi, x).
Axes of the slice: x: 4, y: 4 (y_hi: 2, y_lo: 2; y = y_hi * 2 + y_lo), z: 8, core: 2. Of those that a mesh axis runs over, the one named last changes fastest.
Arguments:
- previous_hidden: bfloat16 [16384, 4096], P('ctx', 'tp'), may hold values from -6 to 6
- output_weight: bfloat16 [4096, 4096], P('tp', 'ctx'), may hold values from -0.09375 to 0.09375
- adapter_down_weight: bfloat16 [4096, 128], P('tp'), may hold values from -0.09375 to 0.09375
- adapter_up_weight: bfloat16 [128, 4096], P('tp'), may hold values from -0.5 to 0.5
- stream: bfloat16 [16384, 4096], P(('ctx', 'tp')), may hold values from -6 to 6
- prenorm_gain: bfloat16 [4096], replicated, may hold values from 0.25 to 1.75
- input_weight: bfloat16 [3, 4096, 4096], P(None, 'ctx', 'tp'), may hold values from -0.09375 to 0.09375
- short_kernel: float32 [3, 7, 4096], P(None, None, 'tp'), may hold values from -2.5 to 2.5
- long_kernel: float32 [128, 4096], P(None, 'tp'), may hold values from -0.5 to 0.5
- long_direct_bias: float32 [4096], P('tp'), may hold values from -6 to 6
Outputs:
- new_stream: bfloat16 [16384, 4096], P(('ctx', 'tp'))
- mixer_out: bfloat16 [16384, 4096], P('ctx', 'tp')
All inputs are finite; a program needn't handle non-finite values.
Results may differ from a plain program's by a relative error of at most 0.012.
Values may be sent and summed in bfloat16 or wider, within the bound.
No kernel may reach another device: no remote copies, remote signals or barrier semaphores. Data moves between devices by JAX's collectives and lax.ppermute only.
A program may use at most 128 MiB of HBM per device.

v0:
```python
import jax
import jax.numpy as jnp
from jax import lax
from jax.sharding import PartitionSpec as P

adapter_scale = 0.5
norm_eps = 1e-05


def passed_along(value, axis, steps):
    count = lax.axis_size(axis)
    leading, last = (max(0, -steps), min(count, count - steps))
    return lax.ppermute(value, axis, [(source, source + steps) for source in range(leading, last)])


def featurize(extended, filters):
    taps = filters.shape[1]
    length = extended.shape[1] - taps + 1
    running = jnp.zeros((extended.shape[0], length, extended.shape[2]), jnp.float32)
    for j in range(taps):
        running = running + filters[:, j, None, :] * extended[
            :, taps - 1 - j : taps - 1 - j + length, :
        ].astype(jnp.float32)
    return running


def long_conv(extended, filters, bias_row):
    taps = filters.shape[0]
    length = extended.shape[0] - taps + 1
    running = bias_row[None, :] * extended[taps - 1 :, :].astype(jnp.float32)
    for j in range(taps):
        running = running + filters[j][None, :] * extended[
            taps - 1 - j : taps - 1 - j + length, :
        ].astype(jnp.float32)
    return running


def normalize(summed, prenorm_gain):
    scale_rows = lax.rsqrt(jnp.mean(summed * summed, axis=1, keepdims=True) + norm_eps)
    return (summed * scale_rows * prenorm_gain.astype(jnp.float32)[None, :]).astype(jnp.bfloat16)


def body(
    previous_hidden,
    output_weight,
    adapter_down_weight,
    adapter_up_weight,
    stream,
    prenorm_gain,
    input_weight,
    short_kernel,
    long_kernel,
    long_direct_bias,
):
    base_term = jnp.dot(
        previous_hidden,
        lax.all_gather(output_weight, "ctx", axis=1, tiled=True),
        preferred_element_type=jnp.float32,
    )
    reduced_rank = jnp.dot(previous_hidden, adapter_down_weight, preferred_element_type=jnp.float32)
    reduced_share = lax.psum_scatter(reduced_rank, "tp", scatter_dimension=1, tiled=True)
    rank_adapter = jnp.dot(
        reduced_share, adapter_up_weight.astype(jnp.float32), precision=lax.Precision.HIGHEST
    )
    partial_sum = base_term + adapter_scale * rank_adapter
    mixed_rows = lax.psum_scatter(partial_sum, "tp", scatter_dimension=0, tiled=True)
    summed = stream.astype(jnp.float32) + mixed_rows
    new_stream = summed.astype(jnp.bfloat16)
    normed = normalize(summed, prenorm_gain)
    token_whole = lax.all_gather(normed, "tp", axis=0, tiled=True)
    projected_sum = jnp.einsum(
        "td,bdc->btc",
        token_whole,
        lax.all_gather(input_weight, "ctx", axis=1, tiled=True),
        preferred_element_type=jnp.float32,
    )
    projected = projected_sum.astype(jnp.bfloat16)
    row_count = projected.shape[1]
    short_taps = short_kernel.shape[1]
    long_taps = long_kernel.shape[0]
    edge_rows = projected[:, row_count - (short_taps - 1) :, :]
    earlier = passed_along(edge_rows, "ctx", 1)
    featured = featurize(jnp.concatenate([earlier, projected], axis=1), short_kernel)
    own_inner = (featured[1] * featured[2]).astype(jnp.bfloat16)
    inner_edge = own_inner[row_count - (long_taps - 1) :, :]
    inner_before = passed_along(inner_edge, "ctx", 1)
    inner_rows = jnp.concatenate([inner_before, own_inner], axis=0)
    leading = featured[0]
    convolved = long_conv(inner_rows, long_kernel, long_direct_bias)
    mixer_out = (leading * convolved).astype(jnp.bfloat16)
    return (new_stream, mixer_out)


def solution(mesh):
    in_specs = (
        P("ctx", "tp"),
        P("tp", "ctx"),
        P("tp", None),
        P("tp", None),
        P(("ctx", "tp"), None),
        P(),
        P(None, "ctx", "tp"),
        P(None, None, "tp"),
        P(None, "tp"),
        P("tp"),
    )
    out_specs = (P(("ctx", "tp"), None), P("ctx", "tp"))
    return jax.shard_map(body, mesh=mesh, in_specs=in_specs, out_specs=out_specs, check_vma=False)
```

profile of v0, /device:TPU:128, one launch (start us, length us, event | category | flops | bytes accessed | tf_op | source)
XLA Modules:
  0.0 425.6 jit_solution(6759283449314921624)
XLA Ops:
  8.1 0.7 all-gather.4.cloned.1.call-update
  8.7 0.0 reduce-scatter.7.cloned.1.call-start
  8.8 0.2 copy-done
  9.0 1.9 convolution_bitcast_fusion
  11.0 0.0 reduce-scatter.5.cloned.1.call-start
  11.1 71.0 %all-gather.4.cloned.1.call-done = bf16[512,4096]{1,0:T(8,128)(2,1)} async-done(((bf16[512,128]{1,0:T(8,128)(2,1)}), bf16[512,4096]{1,0:T(8,128)(2,1)}) %all-gather.4.cloned.1.call-update) | async-done | bytes 4194320 | tf_op jit(solution)/shard_map/all_gather | solution.py:57
  82.1 7.8 %fusion.176 = f32[512,4096]{1,0:T(8,128)} fusion(bf16[512,512]{1,0:T(8,128)(2,1)S(1)} %copy-done, bf16[512,4096]{1,0:T(8,128)(2,1)} %all-gather.4.cloned.1.call-done), kind=kOutput, calls=%fused_computation.328 | convolution fusion | flops 2147483648 | bytes 13107200 | tf_op jit(solution)/shard_map/dot_general | solution.py:55
  89.9 0.7 reduce-scatter.7.cloned.1.call-done
  90.6 8.1 %multiply_add_fusion = f32[512,4096]{1,0:T(8,128)} fusion(f32[512,4096]{1,0:T(8,128)} %fusion.176, bf16[16,4096]{1,0:T(8,128)(2,1)S(1)} %copy-done.4, f32[16,512]{1,0:T(8,128)} %reduce-scatter.7.cloned.1.call-done), kind=kOutput, calls=%fused_computation.126 | convolution fusion | flops 406847488 | bytes 16941056 | tf_op jit(solution)/shard_map/dot_general | solution.py:62
  98.7 0.0 all-gather.8.cloned.1.call-start
  98.8 0.7 all-gather.8.cloned.1.call-update
  99.5 142.4 %reduce-scatter.5.cloned.1.call-done = f32[64,4096]{1,0:T(8,128)} async-done(((f32[512,4096]{1,0:T(8,128)}), f32[64,4096]{1,0:T(8,128)}) %reduce-scatter.5.cloned.1.call-update) | async-done | bytes 1048592 | tf_op jit(solution)/shard_map/reduce_scatter | solution.py:66
  242.0 1.5 multiply_reduce_fusion
  243.5 2.4 multiply_convert_fusion
  246.2 0.6 fusion.172
  246.8 0.7 fusion.173
  247.5 73.6 %all-gather.6.cloned.1.call-done = bf16[512,4096]{1,0:T(8,128)(2,1)} async-done(((bf16[64,4096]{1,0:T(8,128)(2,1)}), bf16[512,4096]{1,0:T(8,128)(2,1)}) %all-gather.6.cloned.1.call-update) | async-done | bytes 4194320 | tf_op jit(solution)/shard_map/all_gather | solution.py:70
  321.0 10.9 %fusion.10 = bf16[3,512,512]{2,1,0:T(8,128)(2,1)S(1)} fusion(bf16[3,4096,512]{2,1,0:T(8,128)(2,1)} %all-gather.8.cloned.1.call-done, bf16[512,4096]{1,0:T(8,128)(2,1)} %all-gather.6.cloned.1.call-done), kind=kOutput, calls=%fused_computation.145 | convolution fusion | flops 6443237376 | bytes 18350080 | tf_op jit(solution)/shard_map/td,bdc->btc/dot_general | solution.py:71
  332.0 1.9 collective-permute-start
  333.9 5.3 %collective-permute-done = bf16[3,6,512]{2,1,0:T(8,128)(2,1)S(1)} collective-permute-done((bf16[3,6,512]{2,1,0:T(8,128)(2,1)S(1)}, bf16[3,6,512]{2,1,0:T(8,128)(2,1)S(1)}, u32[]{:S(2)}, u32[]{:S(2)}) %collective-permute-start) | collective-permute-done | bytes 18464 | tf_op jit(solution)/shard_map/ppermute | solution.py:13
  339.2 2.8 multiply_add_fusion.1
  342.1 0.2 fusion.13
  342.3 2.1 collective-permute-start.1
  344.4 0.2 fusion.183
  344.5 6.1 %collective-permute-done.1 = bf16[127,512]{1,0:T(8,128)(2,1)S(1)} collective-permute-done((bf16[127,512]{1,0:T(8,128)(2,1)S(1)}, bf16[127,512]{1,0:T(8,128)(2,1)S(1)}, u32[]{:S(2)}, u32[]{:S(2)}) %collective-permute-start.1) | collective-permute-done | bytes 130080 | tf_op jit(solution)/shard_map/ppermute | solution.py:13
  350.7 0.5 fusion.163
  351.2 0.7 fusion.157
  351.8 0.7 fusion.151
  352.6 0.7 fusion.145
  353.3 1.6 fusion.139
  354.9 1.9 fusion.133
  356.7 1.9 fusion.127
  358.6 1.9 fusion.121
  360.5 1.8 fusion.115
  362.3 1.9 fusion.109
  364.2 1.9 fusion.103
  366.1 1.9 fusion.97
  368.0 1.9 fusion.91
  369.9 1.9 fusion.85
  371.7 1.9 fusion.79
  373.6 1.9 fusion.73
  375.6 1.9 fusion.67
  377.4 1.9 fusion.61
  379.3 1.8 fusion.55
  381.2 1.9 fusion.49
  383.3 1.8 fusion.43
  385.1 0.3 convert_multiply_fusion.1
  385.7 32.7 %fusion.15 = bf16[512,512]{1,0:T(8,128)(2,1)} fusion(f32[3,512,512]{2,1,0:T(8,128)S(1)} %multiply_add_fusion.1, bf16[512,512]{1,0:T(8,128)(2,1)S(1)} %get-tuple-element.129, bf16[512,512]{1,0:T(8,128)(2,1)S(1)} %get-tuple-element.130, bf16[512,512]{1,0:T(8,128)(2,1)S(1)} %get-tuple-element.128, bf16[512,512]{1,0:T(8,128)(2,1)S(1)} %get-tuple-element.127, ...), kind=kLoop, calls=%fused_computation.151 | loop fusion | flops 100401152 | bytes 71561216 | tf_op jit(solution)/shard_map/convert_element_type | solution.py:90
  (86 shorter events, 0.6 us)
Async XLA Ops:
  8.0 1.1 copy-start
  8.0 74.1 %all-gather.4.cloned.1.call-start = ((), (), s32[]{:S(2)}) async-start(), calls=%async_computation.2 | async-start | bytes 4325376 | tf_op jit(solution)/shard_map/all_gather | solution.py:57
  8.7 81.8 %reduce-scatter.7.cloned.1.call-start = ((), (), s32[]{:S(2)}) async-start(), calls=%async_computation.6 | async-start | bytes 294912
  11.0 79.6 %copy-start.4 = (bf16[16,4096]{1,0:T(8,128)(2,1)S(1)}, bf16[16,4096]{1,0:T(8,128)(2,1)}, u32[]{:S(2)}) copy-start(bf16[16,4096]{1,0:T(8,128)(2,1)} %param.13) | copy-start | bytes 393220
  11.0 231.0 %reduce-scatter.5.cloned.1.call-start = ((), (), s32[]{:S(2)}) async-start(), calls=%async_computation.3 | async-start | bytes 9437184 | tf_op jit(solution)/shard_map/reduce_scatter | solution.py:66
  98.7 0.9 copy-start.31
  98.7 143.3 %copy-start.2 = (bf16[64,4096]{1,0:T(8,128)(2,1)S(1)}, bf16[64,4096]{1,0:T(8,128)(2,1)}, u32[]{:S(2)}) copy-start(bf16[64,4096]{1,0:T(8,128)(2,1)} %param.14) | copy-start | bytes 1572868
  98.7 147.2 %copy-start.5 = (f32[3,7,512]{2,1,0:T(8,128)S(1)}, f32[3,7,512]{2,1,0:T(8,128)}, u32[]{:S(2)}) copy-start(f32[3,7,512]{2,1,0:T(8,128)} %param.17) | copy-start | bytes 129028
  98.7 147.3 %copy-start.3 = (f32[128,512]{1,0:T(8,128)S(1)}, f32[128,512]{1,0:T(8,128)}, u32[]{:S(2)}) copy-start(f32[128,512]{1,0:T(8,128)} %param.18) | copy-start | bytes 786436
  98.7 148.8 %all-gather.8.cloned.1.call-start = ((), (), s32[]{:S(2)}) async-start(), calls=%async_computation.5 | async-start | bytes 12976128 | tf_op jit(solution)/shard_map/all_gather | solution.py:74
  99.5 221.6 %all-gather.6.cloned.1.call-start = ((), (), s32[]{:S(2)}) async-start(), calls=%async_computation.4 | async-start | bytes 4718592 | tf_op jit(solution)/shard_map/all_gather | solution.py:70
  247.5 86.5 %copy-start.32 = (f32[512]{0:T(512)S(1)}, f32[512]{0:T(512)}, u32[]{:S(2)}) copy-start(f32[512]{0:T(512)} %param.19) | copy-start | bytes 6148
  332.0 7.3 %collective-permute-start = (bf16[3,6,512]{2,1,0:T(8,128)(2,1)S(1)}, bf16[3,6,512]{2,1,0:T(8,128)(2,1)S(1)}, u32[]{:S(2)}, u32[]{:S(2)}) collective-permute-start(bf16[3,6,512]{2,1,0:T(8,128)(2,1)S(1)} %slice.1096), channel_id=1, source_target_pairs={{0,8},{8,16},{16,24},{24,32},{32,40},{40,48},{48,56},{56,64},{64,7... | collective-permute-start | bytes 55304 | tf_op jit(solution)/shard_map/ppermute | solution.py:13
  342.3 8.4 %collective-permute-start.1 = (bf16[127,512]{1,0:T(8,128)(2,1)S(1)}, bf16[127,512]{1,0:T(8,128)(2,1)S(1)}, u32[]{:S(2)}, u32[]{:S(2)}) collective-permute-start(bf16[127,512]{1,0:T(8,128)(2,1)S(1)} %slice_bitcast_fusion.1), channel_id=1, source_target_pairs={{0,8},{8,16},{16,24},{24,32},{32,40},{40,48},{48,56},{56,64},{64,7... | collective-permute-start | bytes 390152 | tf_op jit(solution)/shard_map/ppermute | solution.py:13
  383.1 2.4 copy-start.6
  383.1 2.4 copy-start.7
  383.1 2.4 copy-start.8
  383.1 2.4 copy-start.9
  383.1 2.4 copy-start.10
  383.1 2.4 copy-start.11
  383.1 2.4 copy-start.12
  383.1 2.4 copy-start.13
  383.1 2.4 copy-start.14
  383.1 2.4 copy-start.15
  383.1 2.4 copy-start.16
  383.1 2.4 copy-start.17
  383.2 2.4 copy-start.18
  383.2 2.4 copy-start.19
  383.2 2.4 copy-start.20
  383.2 2.4 copy-start.21
  383.2 2.4 copy-start.22
  383.2 2.4 copy-start.23
  383.2 2.4 copy-start.24
  383.2 2.4 copy-start.25
  383.2 2.4 copy-start.26
  383.2 2.4 copy-start.27
  383.3 2.4 copy-start.28
  383.3 2.4 copy-start.29
  383.3 2.4 copy-start.30
  385.7 32.7 %copy-start.1 = (bf16[512,512]{1,0:T(8,128)(2,1)S(1)}, bf16[512,512]{1,0:T(8,128)(2,1)}, u32[]{:S(2)}) copy-start(bf16[512,512]{1,0:T(8,128)(2,1)} %param.10) | copy-start | bytes 1572868
Sparse Core Ops, SparseCore 0:
  10.7 71.3 all-gather.3
  101.6 118.8 all-gather.7
  246.0 74.9 all-gather.5
Sparse Core Ops, SparseCore 1:
  13.6 76.9 reduce-scatter.6
  98.8 143.1 reduce-scatter.4
where the time goes:
time: 426 us
  waiting for transfers between devices  301 us (71%)
  other arithmetic  74.3 us (17%)
  matrix products  28.7 us (7%)
  between operations  15.9 us (4%)
    reduce_scatter x1, waiting for transfers between devices, body(): lax.psum_scatter(partial_sum, 'tp', scatter_dimension=0, tiled=True)  142 us
    all_gather x1, waiting for transfers between devices, body(): token_whole = lax.all_gather(normed, 'tp', axis=0, tiled=True)  73.6 us
    all_gather x1, waiting for transfers between devices, body(): lax.all_gather(output_weight, 'ctx', axis=1, tiled=True)  71 us
    concatenate x21, other arithmetic, body(): inner_rows = jnp.concatenate([inner_before, own_inner], axis=0)  34.2 us
    convert_element_type x1, other arithmetic, body(): mixer_out = (leading * convolved).astype(jnp.bfloat16)  32.7 us
    ppermute x2, waiting for transfers between devices, passed_along(): lax.ppermute(value, axis, [(source, source + steps) for source in range(l...  11.4 us
    dot_general x1, matrix products, body(): jnp.einsum('td,bdc->btc', token_whole, lax.all_gather(input_weight, 'ctx'...  10.9 us
  transfers between devices with their start and end apart: 7, of which 6 were waited for; matrix products, arithmetic and copies ran while one was open for 4% of the time, Pallas kernels for 0%

commit v1 on v0

v1 whole, which is shorter than its diff:
```python
import jax
import jax.numpy as jnp
import ml_dtypes
import numpy as np
from jax import lax
from jax.experimental import pallas as pl
from jax.experimental.pallas import tpu as pltpu
from jax.sharding import PartitionSpec as P

adapter_scale = 0.5
norm_eps = 1e-05
f32 = jnp.float32
bf16 = jnp.bfloat16

NZ, NX = 8, 4
ANY = pl.BlockSpec(memory_space=pl.ANY)
VMEM = pl.BlockSpec(memory_space=pltpu.VMEM)
SMEM = pl.BlockSpec(memory_space=pltpu.SMEM)


def joint(move):
    pairs = []
    for c in range(32):
        for t in range(8):
            z, q, y, x = c // 4, c % 4, t // 4, t % 4
            z2, q2, y2, x2 = move(z, q, y, x)
            pairs.append((c * 8 + t, (z2 * 4 + q2) * 8 + y2 * 4 + x2))
    return pairs


def sign(q):
    return 1 - 2 * (q % 2)


X_A = joint(lambda z, q, y, x: (z, q, y, (x + sign(q)) % NX))
X_B = joint(lambda z, q, y, x: (z, q, y, (x - sign(q)) % NX))
Y_HI = joint(lambda z, q, y, x: (z, q, 1 - y, x))
Z_A = joint(lambda z, q, y, x: ((z + sign(q)) % NZ, q, y, x))
Z_B = joint(lambda z, q, y, x: ((z - sign(q)) % NZ, q, y, x))
CORE = joint(lambda z, q, y, x: (z, q ^ 1, y, x))
Y_LO = joint(lambda z, q, y, x: (z, q ^ 2, y, x))
SWAP = joint(lambda z, q, y, x: (y * 4 + x, q, z // 4, z % 4))


def sent(value, pairs):
    return lax.ppermute(value, ("ctx", "tp"), pairs)


def gather_tp(own):
    a1 = sent(own, X_A)
    b1 = sent(own, X_B)
    y0 = sent(own, Y_HI)
    a2 = sent(a1, X_A)
    ya1 = sent(y0, X_A)
    yb1 = sent(y0, X_B)
    ya2 = sent(ya1, X_A)
    return [own, a1, a2, b1, y0, ya1, ya2, yb1]


def gather_z(own):
    a = [own]
    for _ in range(4):
        a.append(sent(a[-1], Z_A))
    b = [own]
    for _ in range(3):
        b.append(sent(b[-1], Z_B))
    return a + [b[3], b[2], b[1]]


def m1_kernel(idx, *refs):
    hid = refs[:8]
    own = refs[8:16]
    sib = refs[16:24]
    stream, out = refs[24:26]
    a_s, w_s, d_s, u_s, acc, sem_a, sem_w = refs[26:]
    core = idx[16]
    copies = []
    for i in range(8):
        copies.append(pltpu.make_async_copy(hid[i], a_s.at[i], sem_a.at[i]))
    for k in range(8):
        zk = idx[8 + k]
        for part, ref, c in ((0, own[k], core), (1, sib[(8 - k) % 8], 1 - core)):
            for ylo in range(2):
                n = (k * 2 + part) * 2 + ylo
                q = 2 * ylo + c
                copies.append(pltpu.make_async_copy(ref.at[ylo, pl.ds(0, 512)], w_s.at[k, q], sem_w.at[n, 0]))
                copies.append(pltpu.make_async_copy(ref.at[ylo, pl.ds(512, 128)], d_s.at[k, q], sem_w.at[n, 1]))
                copies.append(pltpu.make_async_copy(ref.at[ylo, pl.ds(640, 16)], u_s.at[zk, q], sem_w.at[n, 2]))
    for copy in copies:
        copy.start()
    acc[...] = jnp.zeros_like(acc)
    for copy in copies:
        copy.wait()

    def step(k, carry):
        w = jnp.concatenate([w_s[k, 0], w_s[k, 1], w_s[k, 2], w_s[k, 3], d_s[k].reshape(512, 128)], axis=1)
        acc[...] += jnp.dot(a_s[idx[k]], w, preferred_element_type=f32)
        return carry

    lax.fori_loop(0, 8, step, 0)
    low = acc[:, 512:]
    for q in range(4):
        up = u_s[:, q].reshape(128, 128).astype(f32)
        term = jnp.dot(low, up, precision=lax.Precision.HIGHEST, preferred_element_type=f32)
        cols = slice(128 * q, 128 * q + 128)
        out[:, cols] = (stream[:, cols].astype(f32) + (acc[:, cols] + adapter_scale * term)).astype(bf16)


def m1(idx, hid, own, sib, stream):
    return pl.pallas_call(
        m1_kernel,
        out_shape=jax.ShapeDtypeStruct((512, 512), bf16),
        in_specs=[SMEM] + [ANY] * 24 + [VMEM],
        out_specs=VMEM,
        scratch_shapes=[
            pltpu.VMEM((8, 512, 512), bf16),
            pltpu.VMEM((8, 4, 512, 128), bf16),
            pltpu.VMEM((8, 4, 128, 128), bf16),
            pltpu.VMEM((8, 4, 16, 128), bf16),
            pltpu.VMEM((512, 640), f32),
            pltpu.SemaphoreType.DMA((8,)),
            pltpu.SemaphoreType.DMA((32, 3)),
        ],
        compiler_params=pltpu.CompilerParams(vmem_limit_bytes=40 * 2**20),
        cost_estimate=pl.CostEstimate(flops=2 * 512 * 4096 * 640, bytes_accessed=12 * 2**20, transcendentals=0),
        name="m1",
    )(idx, *hid, *own, *sib, stream)


def m2_kernel(idx, *refs):
    blocks = refs[:8]
    gain, w_in = refs[8:10]
    proj, new_stream = refs[10:12]
    a_s, n_s, w_s, acc, sem_a, sem_w, sem_o = refs[12:]
    a_copies = [pltpu.make_async_copy(blocks[i], a_s.at[i], sem_a.at[i]) for i in range(8)]
    w_copies = [pltpu.make_async_copy(w_in.at[pl.ds(4 * k, 4)], w_s.at[k], sem_w.at[k]) for k in range(8)]
    for copy in a_copies + w_copies:
        copy.start()
    total = jnp.zeros((512, 128), f32)
    for i in range(8):
        a_copies[i].wait()
        block = a_s[i].astype(f32)
        square = block * block
        total += square[:, :128] + square[:, 128:256] + square[:, 256:384] + square[:, 384:]
    rows = pl.multiple_of(64 * idx[9], 64)
    o_copies = [
        pltpu.make_async_copy(a_s.at[idx[k], pl.ds(rows, 64)], new_stream.at[:, pl.ds(512 * k, 512)], sem_o.at[k])
        for k in range(8)
    ]
    for copy in o_copies:
        copy.start()
    scale = lax.rsqrt(jnp.sum(total, axis=1, keepdims=True) * (1.0 / 4096) + norm_eps)
    for k in range(8):
        n_s[k] = (a_s[idx[k]].astype(f32) * scale * gain[:, 512 * k : 512 * k + 512].astype(f32)).astype(bf16)
    acc[...] = jnp.zeros_like(acc)
    for copy in w_copies:
        copy.wait()

    def step(k, carry):
        a = n_s[k]
        for b in range(3):
            acc[b] += jnp.dot(a, w_s[k, :, b].reshape(512, 512), preferred_element_type=f32)
        return carry

    lax.fori_loop(0, 8, step, 0)
    proj[...] = acc[...].astype(bf16)
    for copy in o_copies:
        copy.wait()


def m2(idx, blocks, gain, w_in):
    return pl.pallas_call(
        m2_kernel,
        out_shape=[jax.ShapeDtypeStruct((3, 512, 512), bf16), jax.ShapeDtypeStruct((64, 4096), bf16)],
        in_specs=[SMEM] + [ANY] * 8 + [VMEM, ANY],
        out_specs=[VMEM, ANY],
        scratch_shapes=[
            pltpu.VMEM((8, 512, 512), bf16),
            pltpu.VMEM((8, 512, 512), bf16),
            pltpu.VMEM((8, 4, 3, 128, 512), bf16),
            pltpu.VMEM((3, 512, 512), f32),
            pltpu.SemaphoreType.DMA((8,)),
            pltpu.SemaphoreType.DMA((8,)),
            pltpu.SemaphoreType.DMA((8,)),
        ],
        compiler_params=pltpu.CompilerParams(vmem_limit_bytes=50 * 2**20),
        cost_estimate=pl.CostEstimate(flops=2 * 512 * 4096 * 1536, bytes_accessed=20 * 2**20, transcendentals=0),
        name="m2",
    )(idx, *blocks, gain, w_in)


def dft_tables():
    n = np.arange(256, dtype=np.int64)
    k = np.arange(128, dtype=np.int64)
    angle = (2 * np.pi / 256) * ((k[:, None] * n[None, :]) % 256)
    cos, sin = np.cos(angle), np.sin(angle)
    sin[0] = np.cos(np.pi * n)
    forward = np.concatenate([cos, sin])
    weight = np.full((128, 1), 2.0)
    weight[0] = 1.0
    inverse = (np.concatenate([cos * weight, sin * weight]) / 256.0).T[128:]
    return split_np(forward) + split_np(inverse)


def split_np(table):
    high = table.astype(np.float32).astype(ml_dtypes.bfloat16)
    low = (table - high.astype(np.float64)).astype(np.float32).astype(ml_dtypes.bfloat16)
    return [high, low]


def split(value):
    high = value.astype(bf16)
    return high, (value - high.astype(f32)).astype(bf16)


def dot(a, b):
    return jnp.dot(a, b, preferred_element_type=f32)


def conv_kernel(inner, halo, lead, taps, bias, f_hi, f_lo, g_hi, g_lo, out):
    row = lax.broadcasted_iota(jnp.int32, (128, 512), 0)
    first = row == 0
    h = taps[...] + jnp.where(first, bias[...], 0.0)
    h_hi, h_lo = split(h)
    fh, fl = f_hi[:, :128], f_lo[:, :128]
    spectrum = dot(fh, h_hi) + dot(fh, h_lo) + dot(fl, h_hi)
    h_a, h_b = spectrum[:128], spectrum[128:]
    mixed = jnp.where(first, 0.0, h_b)
    last = jnp.where(first, h_b, h_a)
    for w in range(4):
        if w == 0:
            window = jnp.concatenate([halo[...], inner[:128]], axis=0)
        else:
            window = inner[128 * (w - 1) : 128 * (w + 1)]
        x = dot(f_hi[...], window) + dot(f_lo[...], window)
        x_a, x_b = x[:128], x[128:]
        y_hi, y_lo = split(jnp.concatenate([x_a * h_a - x_b * mixed, x_a * mixed + x_b * last], axis=0))
        y = dot(g_hi[...], y_hi) + dot(g_hi[...], y_lo) + dot(g_lo[...], y_hi)
        rows = slice(128 * w, 128 * w + 128)
        out[rows] = (lead[rows] * y).astype(bf16)


def conv(inner, halo, lead, taps, bias):
    tables = [jnp.asarray(t) for t in dft_tables()]
    return pl.pallas_call(
        conv_kernel,
        out_shape=jax.ShapeDtypeStruct((512, 512), bf16),
        in_specs=[VMEM] * 9,
        out_specs=VMEM,
        compiler_params=pltpu.CompilerParams(vmem_limit_bytes=40 * 2**20),
        cost_estimate=pl.CostEstimate(flops=10**9, bytes_accessed=4 * 2**20, transcendentals=0),
        name="conv",
    )(inner, halo, lead, taps, bias, *tables)


def passed_along(value):
    return lax.ppermute(value, "ctx", [(c, c + 1) for c in range(31)])


def featurize(extended, filters):
    taps = filters.shape[1]
    length = extended.shape[1] - taps + 1
    running = jnp.zeros((extended.shape[0], length, extended.shape[2]), f32)
    for j in range(taps):
        running = running + filters[:, j, None, :] * extended[:, taps - 1 - j : taps - 1 - j + length, :].astype(f32)
    return running


def body(
    previous_hidden,
    output_weight,
    adapter_down_weight,
    adapter_up_weight,
    stream,
    prenorm_gain,
    input_weight,
    short_kernel,
    long_kernel,
    long_direct_bias,
):
    c = lax.axis_index("ctx")
    t = lax.axis_index("tp")
    z, q, core = c // 4, c % 4, c % 2
    y, x = t // 4, t % 4
    s = 1 - 2 * core

    def slot_of(block):
        return 4 * ((block // 4) ^ y) + (s * (x - block % 4)) % 4

    near = (z - s * jnp.arange(8, dtype=jnp.int32)) % 8
    idx1 = jnp.concatenate([slot_of(near), near, core[None]]).astype(jnp.int32)
    idx2 = jnp.concatenate([slot_of(jnp.arange(8, dtype=jnp.int32)), core[None], t[None]]).astype(jnp.int32)

    w_in = lax.all_gather(input_weight, "ctx", axis=0, tiled=False)
    down = lax.dynamic_slice_in_dim(adapter_down_weight, 128 * q, 128, axis=0)
    up = lax.dynamic_slice_in_dim(adapter_up_weight, 128 * c, 128, axis=1)
    weights = sent(jnp.concatenate([output_weight, down, up], axis=0), SWAP)
    hid = gather_tp(previous_hidden)
    other = sent(weights, Y_LO)
    low = (q // 2) == 0
    both = jnp.stack([jnp.where(low, weights, other), jnp.where(low, other, weights)])
    own = gather_z(both)
    sib = [sent(value, CORE) for value in own]
    stream_cols = lax.all_to_all(stream, "tp", split_axis=1, concat_axis=0, tiled=True)
    block = m1(idx1, hid, own, sib, stream_cols)
    blocks = gather_tp(block)
    projected, new_stream = m2(idx2, blocks, prenorm_gain.reshape(1, 4096), w_in)

    earlier = passed_along(projected[:, 506:, :])
    featured = featurize(jnp.concatenate([earlier, projected], axis=1), short_kernel)
    inner = (featured[1] * featured[2]).astype(bf16)
    halo = passed_along(inner[384:])
    mixer_out = conv(inner, halo, featured[0], long_kernel, long_direct_bias.reshape(1, 512))
    return (new_stream, mixer_out)


def solution(mesh):
    in_specs = (
        P("ctx", "tp"),
        P("tp", "ctx"),
        P("tp", None),
        P("tp", None),
        P(("ctx", "tp"), None),
        P(),
        P(None, "ctx", "tp"),
        P(None, None, "tp"),
        P(None, "tp"),
        P("tp"),
    )
    out_specs = (P(("ctx", "tp"), None), P("ctx", "tp"))
    return jax.shard_map(body, mesh=mesh, in_specs=in_specs, out_specs=out_specs, check_vma=False)
```

time: 426 us -> 236 us (0.55)
  waiting for transfers between devices: 301 us -> 95.1 us
  other arithmetic: 74.3 us -> 8.78 us
  starting transfers between devices: 4.23 us -> 68.9 us
  Pallas kernels: 0 us -> 31 us
  matrix products: 28.7 us -> 0 us
  local copies, waits for them, and re-layouts: 1.94 us -> 14 us
    all_gather x3 -> x1, waiting for transfers between devices: 145 us -> 0.01 us  [body(): w_in = lax.all_gather(input_weight, 'ctx', axis=0, tiled=False)]
    reduce_scatter x1 -> x0, waiting for transfers between devices: 142 us -> none  [body(): lax.psum_scatter(partial_sum, 'tp', scatter_dimension=0, tiled=True)]
    ppermute x2 -> x33, waiting for transfers between devices: 11.4 us -> 85.4 us  [the longest x31 73.7 us: sent(): return lax.ppermute(value, ('ctx', 'tp'), pairs)]
    ppermute x2 -> x33, starting transfers between devices: 4.02 us -> 63.6 us  [the longest x31 59.8 us: sent(): return lax.ppermute(value, ('ctx', 'tp'), pairs)]
    convert_element_type x5 -> x0, other arithmetic: 35.4 us -> none  [the longest x1 32.7 us: body(): mixer_out = (leading * convolved).astype(jnp.bfloat16)]
    concatenate x21 -> x3, other arithmetic: 34.2 us -> 1.07 us  [the longest x1 0.92 us: body(): weights = sent(jnp.concatenate([output_weight, down, up], axis=0), SWAP)]
    pallas_call x0 -> x3, Pallas kernels: none -> 31 us  [the longest x1 16.8 us: m2(): pl.pallas_call(m2_kernel, out_shape=[jax.ShapeDtypeStruct((3, 512, 512),...]
    dot_general x3 -> x0, matrix products: 26.8 us -> none  [the longest x1 10.9 us: body(): jnp.einsum('td,bdc->btc', token_whole, lax.all_gather(input_weight, 'ctx'...]
  transfers between devices with their start and end apart: 7 -> 35, of which waited for: 6 -> 12; matrix products, arithmetic and copies ran while one was open for 4% -> 2% of each run, Pallas kernels for 0% -> 5%
where the time goes in v1:
time: 236 us; the launch traced here: 232 us
  waiting for transfers between devices  95.1 us (40%)
  starting transfers between devices  68.9 us (29%)
  Pallas kernels  31 us (13%)
  between operations  14.4 us (6%)
  local copies, waits for them, and re-layouts  14 us (6%)
  other arithmetic  8.78 us (4%)
    ppermute x31, waiting for transfers between devices, sent(): return lax.ppermute(value, ('ctx', 'tp'), pairs)  73.7 us
    ppermute x31, starting transfers between devices, sent(): return lax.ppermute(value, ('ctx', 'tp'), pairs)  59.8 us
    pallas_call x1, Pallas kernels, m2(): pl.pallas_call(m2_kernel, out_shape=[jax.ShapeDtypeStruct((3, 512, 512),...  16.8 us
    ppermute x2, waiting for transfers between devices, passed_along(): return lax.ppermute(value, 'ctx', [(c, c + 1) for c in range(31)])  11.8 us
    pallas_call x1, Pallas kernels, m1(): pl.pallas_call(m1_kernel, out_shape=jax.ShapeDtypeStruct((512, 512), bf16...  11.3 us
    unnamed x50, local copies, waits for them, and re-layouts  10.6 us
    all_to_all x1, waiting for transfers between devices, body(): lax.all_to_all(stream, 'tp', split_axis=1, concat_axis=0, tiled=True)  8.96 us
    add x1, other arithmetic, featurize(): running + filters[:, j, None, :] * extended[:, taps - 1 - j:taps - 1 - j...  7.37 us
  transfers between devices with their start and end apart: 35, of which 12 were waited for; matrix products, arithmetic and copies ran while one was open for 2% of the time, Pallas kernels for 5%

profile of v1, /device:TPU:128, one launch (start us, length us, event | category | flops | bytes accessed | tf_op | source)
XLA Modules:
  0.0 232.2 jit_solution(8443009185223616529)
XLA Ops:
  8.6 0.9 pad_maximum_fusion.2
  9.6 3.3 %collective-permute-start.7 = (bf16[656,128]{1,0:T(8,128)(2,1)S(1)}, bf16[656,128]{1,0:T(8,128)(2,1)S(1)}, u32[]{:S(2)}, u32[]{:S(2)}) collective-permute-start(bf16[656,128]{1,0:T(8,128)(2,1)S(1)} %pad_maximum_fusion.2), channel_id=1, source_target_pairs={{0,0},{1,32},{2,64},{3,96},{4,128},{5,160},{6,192},{7,224},{8,8},{... | collective-permute-start | bytes 503816 | tf_op jit(solution)/shard_map/ppermute | solution.py:46
  12.9 11.2 %collective-permute-done.7 = bf16[656,128]{1,0:T(8,128)(2,1)S(1)} collective-permute-done((bf16[656,128]{1,0:T(8,128)(2,1)S(1)}, bf16[656,128]{1,0:T(8,128)(2,1)S(1)}, u32[]{:S(2)}, u32[]{:S(2)}) %collective-permute-start.7) | collective-permute-done | bytes 167968 | tf_op jit(solution)/shard_map/ppermute | solution.py:46
  24.1 1.6 collective-permute-start.8
  25.7 9.1 %collective-permute-start = (bf16[512,512]{1,0:T(8,128)(2,1)}, bf16[512,512]{1,0:T(8,128)(2,1)S(1)}, u32[]{:S(2)}, u32[]{:S(2)}) collective-permute-start(bf16[512,512]{1,0:T(8,128)(2,1)} %refs_0_.1), channel_id=1, source_target_pairs={{0,1},{1,2},{2,3},{3,0},{4,5},{5,6},{6,7},{7,4},{8,11},{9,8},{10,9... | collective-permute-start | bytes 1572872 | tf_op jit(solution)/shard_map/ppermute | solution.py:46
  34.8 7.2 %collective-permute-start.2 = (bf16[512,512]{1,0:T(8,128)(2,1)}, bf16[512,512]{1,0:T(8,128)(2,1)S(1)}, u32[]{:S(2)}, u32[]{:S(2)}) collective-permute-start(bf16[512,512]{1,0:T(8,128)(2,1)} %refs_0_.1), channel_id=1, source_target_pairs={{0,3},{1,0},{2,1},{3,2},{4,7},{5,4},{6,5},{7,6},{8,9},{9,10},{10,1... | collective-permute-start | bytes 1572872 | tf_op jit(solution)/shard_map/ppermute | solution.py:46
  42.1 3.2 %collective-permute-start.13 = (bf16[2,656,128]{2,1,0:T(8,128)(2,1)S(1)}, bf16[2,656,128]{2,1,0:T(8,128)(2,1)S(1)}, u32[]{:S(2)}, u32[]{:S(2)}) collective-permute-start(bf16[2,656,128]{2,1,0:T(8,128)(2,1)S(1)} %pad_maximum_fusion.1.refs_8_), channel_id=1, source_target_pairs={{0,224},{1,225},{2,226},{3,227},{4,228},{5,229},{6,230},{7,231},{8... | collective-permute-start | bytes 1007624 | tf_op jit(solution)/shard_map/ppermute | solution.py:46
  45.3 14.8 %collective-permute-done.9.refs_9_ = bf16[2,656,128]{2,1,0:T(8,128)(2,1)S(1)} collective-permute-done((bf16[2,656,128]{2,1,0:T(8,128)(2,1)S(1)}, bf16[2,656,128]{2,1,0:T(8,128)(2,1)S(1)}, u32[]{:S(2)}, u32[]{:S(2)}) %collective-permute-start.9) | collective-permute-done | bytes 335904 | tf_op jit(solution)/shard_map/ppermute | solution.py:46
  60.2 3.2 %collective-permute-start.14 = (bf16[2,656,128]{2,1,0:T(8,128)(2,1)S(1)}, bf16[2,656,128]{2,1,0:T(8,128)(2,1)}, u32[]{:S(2)}, u32[]{:S(2)}) collective-permute-start(bf16[2,656,128]{2,1,0:T(8,128)(2,1)S(1)} %collective-permute-done.13.refs_15_), channel_id=1, source_target_pairs={{0,224},{1,225},{2,226},{3,227},{4,228},{5,229},{6,230},{7,231},{8... | collective-permute-start | bytes 1007624 | tf_op jit(solution)/shard_map/ppermute | solution.py:46
  64.3 5.4 %collective-permute-start.6 = (bf16[512,512]{1,0:T(8,128)(2,1)S(1)}, bf16[512,512]{1,0:T(8,128)(2,1)S(1)}, u32[]{:S(2)}, u32[]{:S(2)}) collective-permute-start(bf16[512,512]{1,0:T(8,128)(2,1)S(1)} %collective-permute-done.3.refs_4_), channel_id=1, source_target_pairs={{0,3},{1,0},{2,1},{3,2},{4,7},{5,4},{6,5},{7,6},{8,9},{9,10},{10,1... | collective-permute-start | bytes 1572872 | tf_op jit(solution)/shard_map/ppermute | solution.py:46
  69.6 6.3 %collective-permute-done.10.refs_10_ = bf16[2,656,128]{2,1,0:T(8,128)(2,1)} collective-permute-done((bf16[2,656,128]{2,1,0:T(8,128)(2,1)S(1)}, bf16[2,656,128]{2,1,0:T(8,128)(2,1)}, u32[]{:S(2)}, u32[]{:S(2)}) %collective-permute-start.10) | collective-permute-done | bytes 335904 | tf_op jit(solution)/shard_map/ppermute | solution.py:46
  76.0 0.7 copy-done.6
  76.7 1.1 collective-permute-start.11
  77.8 0.7 copy-done.10
  78.6 1.9 collective-permute-start.1
  81.2 1.3 collective-permute-start.15
  82.5 4.0 %collective-permute-start.18 = (bf16[2,656,128]{2,1,0:T(8,128)(2,1)}, bf16[2,656,128]{2,1,0:T(8,128)(2,1)}, u32[]{:S(2)}, u32[]{:S(2)}) collective-permute-start(bf16[2,656,128]{2,1,0:T(8,128)(2,1)} %collective-permute-done.10.refs_10_), channel_id=1, source_target_pairs={{0,8},{1,9},{2,10},{3,11},{4,12},{5,13},{6,14},{7,15},{8,0},{9,1},... | collective-permute-start | bytes 1007624 | tf_op jit(solution)/shard_map/ppermute | solution.py:46
  86.4 7.0 %collective-permute-done.11.refs_11_ = bf16[2,656,128]{2,1,0:T(8,128)(2,1)} collective-permute-done((bf16[2,656,128]{2,1,0:T(8,128)(2,1)}, bf16[2,656,128]{2,1,0:T(8,128)(2,1)}, u32[]{:S(2)}, u32[]{:S(2)}) %collective-permute-start.11) | collective-permute-done | bytes 335904 | tf_op jit(solution)/shard_map/ppermute | solution.py:46
  93.5 2.5 %collective-permute-start.12 = (bf16[2,656,128]{2,1,0:T(8,128)(2,1)}, bf16[2,656,128]{2,1,0:T(8,128)(2,1)}, u32[]{:S(2)}, u32[]{:S(2)}) collective-permute-start(bf16[2,656,128]{2,1,0:T(8,128)(2,1)} %collective-permute-done.11.refs_11_), channel_id=1, source_target_pairs={{0,32},{1,33},{2,34},{3,35},{4,36},{5,37},{6,38},{7,39},{8,232},{9... | collective-permute-start | bytes 1007624 | tf_op jit(solution)/shard_map/ppermute | solution.py:46
  96.0 7.1 %collective-permute-start.5 = (bf16[512,512]{1,0:T(8,128)(2,1)}, bf16[512,512]{1,0:T(8,128)(2,1)}, u32[]{:S(2)}, u32[]{:S(2)}) collective-permute-start(bf16[512,512]{1,0:T(8,128)(2,1)} %collective-permute-done.4.refs_5_), channel_id=1, source_target_pairs={{0,1},{1,2},{2,3},{3,0},{4,5},{5,6},{6,7},{7,4},{8,11},{9,8},{10,9... | collective-permute-start | bytes 1572872 | tf_op jit(solution)/shard_map/ppermute | solution.py:46
  103.1 1.9 copy.35
  105.0 5.3 %all-to-all-start = ((bf16[64,8,512]{2,0,1:T(8,128)(2,1)}), bf16[64,8,512]{2,0,1:T(8,128)(2,1)S(1)}, u32[]{:S(2)}, u32[]{:S(2)}) async-start(bf16[64,8,512]{2,0,1:T(8,128)(2,1)} %bitcast.38), calls=%async_computation | async-start | bytes 1048576 | tf_op jit(solution)/shard_map/all_to_all | solution.py:304
  111.5 9.0 %all-to-all-done = bf16[64,8,512]{2,0,1:T(8,128)(2,1)S(1)} async-done(((bf16[64,8,512]{2,0,1:T(8,128)(2,1)}), bf16[64,8,512]{2,0,1:T(8,128)(2,1)S(1)}, u32[]{:S(2)}, u32[]{:S(2)}) %all-to-all-start) | async-done | bytes 524320 | tf_op jit(solution)/shard_map/all_to_all | solution.py:304
  120.5 1.0 copy-done.3
  121.5 1.0 copy-done.7
  122.5 1.0 copy-done.9
  123.5 1.0 copy-done.11
  124.5 1.0 copy-done.13
  125.4 11.3 %m1.1.refs_0_ = bf16[512,512]{1,0:T(8,128)(2,1)S(1)} custom-call(s32[17]{0:T(128)S(1)} %pad_add_fusion.1.idx, bf16[512,512]{1,0:T(8,128)(2,1)S(1)} %copy-done.1, bf16[512,512]{1,0:T(8,128)(2,1)S(1)} %collective-permute-done.refs_1_, bf16[512,512]{1,0:T(8,128)(2,1)} %collective-permute-done.1.refs_2_, bf16[512,512]{1,0:T(8,128)(2,1)S(1)} %collective-permute-done.2.refs_3_, ...), custom_call_target="tpu_custom_call" | custom-call | flops 2684354560 | bytes 12582912 | tf_op jit(solution)/shard_map/m1/pallas_call | solution.py:110
  137.4 1.2 collective-permute-start.24
  138.5 9.0 %collective-permute-done.27.refs_4_ = bf16[512,512]{1,0:T(8,128)(2,1)S(1)} collective-permute-done((bf16[512,512]{1,0:T(8,128)(2,1)S(1)}, bf16[512,512]{1,0:T(8,128)(2,1)S(1)}, u32[]{:S(2)}, u32[]{:S(2)}) %collective-permute-start.27) | collective-permute-done | bytes 524320 | tf_op jit(solution)/shard_map/ppermute | solution.py:46
  147.5 1.1 collective-permute-start.28
  148.7 2.8 %collective-permute-start.26 = (bf16[512,512]{1,0:T(8,128)(2,1)S(1)}, bf16[512,512]{1,0:T(8,128)(2,1)S(1)}, u32[]{:S(2)}, u32[]{:S(2)}) collective-permute-start(bf16[512,512]{1,0:T(8,128)(2,1)S(1)} %m1.1.refs_0_), channel_id=1, source_target_pairs={{0,3},{1,0},{2,1},{3,2},{4,7},{5,4},{6,5},{7,6},{8,9},{9,10},{10,1... | collective-permute-start | bytes 1572872 | tf_op jit(solution)/shard_map/ppermute | solution.py:46
  151.5 0.8 copy-done.4
  152.3 2.0 collective-permute-start.30
  154.3 9.7 %collective-permute-done.28.refs_5_ = bf16[512,512]{1,0:T(8,128)(2,1)S(1)} collective-permute-done((bf16[512,512]{1,0:T(8,128)(2,1)S(1)}, bf16[512,512]{1,0:T(8,128)(2,1)S(1)}, u32[]{:S(2)}, u32[]{:S(2)}) %collective-permute-start.28) | collective-permute-done | bytes 524320 | tf_op jit(solution)/shard_map/ppermute | solution.py:46
  164.1 10.7 %collective-permute-done.25.refs_2_ = bf16[512,512]{1,0:T(8,128)(2,1)S(1)} collective-permute-done((bf16[512,512]{1,0:T(8,128)(2,1)S(1)}, bf16[512,512]{1,0:T(8,128)(2,1)S(1)}, u32[]{:S(2)}, u32[]{:S(2)}) %collective-permute-start.25) | collective-permute-done | bytes 524320 | tf_op jit(solution)/shard_map/ppermute | solution.py:46
  175.1 0.8 copy-done.22
  175.9 4.5 %collective-permute-done.29.refs_6_ = bf16[512,512]{1,0:T(8,128)(2,1)S(1)} collective-permute-done((bf16[512,512]{1,0:T(8,128)(2,1)S(1)}, bf16[512,512]{1,0:T(8,128)(2,1)S(1)}, u32[]{:S(2)}, u32[]{:S(2)}) %collective-permute-start.29) | collective-permute-done | bytes 524320 | tf_op jit(solution)/shard_map/ppermute | solution.py:46
  180.4 1.0 copy-done.5
  181.5 16.8 %m2.1 = (bf16[3,512,512]{2,1,0:T(8,128)(2,1)}, bf16[64,4096]{1,0:T(8,128)(2,1)}) custom-call(s32[10]{0:T(128)S(1)} %pad_add_fusion.idx, bf16[512,512]{1,0:T(8,128)(2,1)S(1)} %copy-done.5, bf16[512,512]{1,0:T(8,128)(2,1)S(1)} %collective-permute-done.24.refs_1_, bf16[512,512]{1,0:T(8,128)(2,1)S(1)} %collective-permute-done.25.refs_2_, ...), custom_call_target="tpu_custom_call" | custom-call | flops 6442450944 | bytes 20971520 | tf_op jit(solution)/shard_map/m2/pallas_call | solution.py:172
  198.2 0.7 slice.59
  199.0 1.9 collective-permute-start.31
  200.9 5.3 %collective-permute-done.31 = bf16[3,6,512]{2,1,0:T(8,128)(2,1)S(1)} collective-permute-done((bf16[3,6,512]{2,1,0:T(8,128)(2,1)S(1)}, bf16[3,6,512]{2,1,0:T(8,128)(2,1)S(1)}, u32[]{:S(2)}, u32[]{:S(2)}) %collective-permute-start.31) | collective-permute-done | bytes 18464 | tf_op jit(solution)/shard_map/ppermute | solution.py:257
  206.2 7.4 %multiply_add_fusion = f32[3,512,512]{2,1,0:T(8,128)S(1)} fusion(bf16[3,512,512]{2,1,0:T(8,128)(2,1)} %get-tuple-element.5, bf16[3,6,512]{2,1,0:T(8,128)(2,1)S(1)} %collective-permute-done.31, f32[3,512]{1,0:T(4,128)S(1)} %get-tuple-element.19, f32[3,512]{1,0:T(4,128)S(1)} %get-tuple-element.20, f32[3,512]{1,0:T(4,128)S(1)} %get-tuple-element.21, ...), kind=kLoop, calls=%fused_computation.5 | loop fusion | flops 29884416 | bytes 4780032 | tf_op jit(solution)/shard_map/add | solution.py:265
  214.0 1.9 collective-permute-start.32
  215.9 6.5 %collective-permute-done.32.halo = bf16[128,512]{1,0:T(8,128)(2,1)S(1)} collective-permute-done((bf16[128,512]{1,0:T(8,128)(2,1)S(1)}, bf16[128,512]{1,0:T(8,128)(2,1)S(1)}, u32[]{:S(2)}, u32[]{:S(2)}) %collective-permute-start.32) | collective-permute-done | bytes 131104 | tf_op jit(solution)/shard_map/ppermute | solution.py:257
  222.4 2.9 %conv.1 = bf16[512,512]{1,0:T(8,128)(2,1)} custom-call(bf16[512,512]{1,0:T(8,128)(2,1)S(1)} %bitcast.36, bf16[128,512]{1,0:T(8,128)(2,1)S(1)} %collective-permute-done.32.halo, f32[512,512]{1,0:T(8,128)S(1)} %get-tuple-element.6.lead, f32[128,512]{1,0:T(8,128)S(1)} %copy-done.14, f32[1,512]{1,0:T(1,128)S(1)} %bitcast.37, bf16[256,256]{1,0:T(8,128)(2,1)S(1)} %copy-done.16, ...), custom_call_target="tpu_custom_call" | custom-call | flops 1000000000 | bytes 4194304 | tf_op jit(solution)/shard_map/conv/pallas_call | solution.py:245
  (92 shorter events, 5.8 us)
Async XLA Ops:
  7.2 1.5 copy-start
  7.2 113.3 %copy-start.1 = (bf16[512,512]{1,0:T(8,128)(2,1)S(1)}, bf16[512,512]{1,0:T(8,128)(2,1)}, u32[]{:S(2)}) copy-start(bf16[512,512]{1,0:T(8,128)(2,1)} %refs_0_.1) | copy-start | bytes 1572868
  7.2 173.2 %all-gather.3.cloned.1.call-start = ((), (), s32[]{:S(2)}) async-start(), calls=%async_computation.1 | async-start | bytes 12976128 | tf_op jit(solution)/shard_map/all_gather | solution.py:294
  9.6 14.5 %collective-permute-start.7 = (bf16[656,128]{1,0:T(8,128)(2,1)S(1)}, bf16[656,128]{1,0:T(8,128)(2,1)S(1)}, u32[]{:S(2)}, u32[]{:S(2)}) collective-permute-start(bf16[656,128]{1,0:T(8,128)(2,1)S(1)} %pad_maximum_fusion.2), channel_id=1, source_target_pairs={{0,0},{1,32},{2,64},{3,96},{4,128},{5,160},{6,192},{7,224},{8,8},{... | collective-permute-start | bytes 503816 | tf_op jit(solution)/shard_map/ppermute | solution.py:46
  24.1 17.8 %collective-permute-start.8 = (bf16[656,128]{1,0:T(8,128)(2,1)S(1)}, bf16[656,128]{1,0:T(8,128)(2,1)S(1)}, u32[]{:S(2)}, u32[]{:S(2)}) collective-permute-start(bf16[656,128]{1,0:T(8,128)(2,1)S(1)} %collective-permute-done.7), channel_id=1, source_target_pairs={{0,16},{1,17},{2,18},{3,19},{4,20},{5,21},{6,22},{7,23},{8,24},{9,... | collective-permute-start | bytes 503816 | tf_op jit(solution)/shard_map/ppermute | solution.py:46
  25.7 19.7 %collective-permute-start.3 = (bf16[512,512]{1,0:T(8,128)(2,1)}, bf16[512,512]{1,0:T(8,128)(2,1)S(1)}, u32[]{:S(2)}, u32[]{:S(2)}) collective-permute-start(bf16[512,512]{1,0:T(8,128)(2,1)} %refs_0_.1), channel_id=1, source_target_pairs={{0,4},{1,5},{2,6},{3,7},{4,0},{5,1},{6,2},{7,3},{8,12},{9,13},{10,... | collective-permute-start | bytes 1572872 | tf_op jit(solution)/shard_map/ppermute | solution.py:46
  25.7 37.7 %collective-permute-start = (bf16[512,512]{1,0:T(8,128)(2,1)}, bf16[512,512]{1,0:T(8,128)(2,1)S(1)}, u32[]{:S(2)}, u32[]{:S(2)}) collective-permute-start(bf16[512,512]{1,0:T(8,128)(2,1)} %refs_0_.1), channel_id=1, source_target_pairs={{0,1},{1,2},{2,3},{3,0},{4,5},{5,6},{6,7},{7,4},{8,11},{9,8},{10,9... | collective-permute-start | bytes 1572872 | tf_op jit(solution)/shard_map/ppermute | solution.py:46
  34.8 28.7 %collective-permute-start.2 = (bf16[512,512]{1,0:T(8,128)(2,1)}, bf16[512,512]{1,0:T(8,128)(2,1)S(1)}, u32[]{:S(2)}, u32[]{:S(2)}) collective-permute-start(bf16[512,512]{1,0:T(8,128)(2,1)} %refs_0_.1), channel_id=1, source_target_pairs={{0,3},{1,0},{2,1},{3,2},{4,7},{5,4},{6,5},{7,6},{8,9},{9,10},{10,1... | collective-permute-start | bytes 1572872 | tf_op jit(solution)/shard_map/ppermute | solution.py:46
  42.0 18.1 %collective-permute-start.9 = (bf16[2,656,128]{2,1,0:T(8,128)(2,1)S(1)}, bf16[2,656,128]{2,1,0:T(8,128)(2,1)S(1)}, u32[]{:S(2)}, u32[]{:S(2)}) collective-permute-start(bf16[2,656,128]{2,1,0:T(8,128)(2,1)S(1)} %pad_maximum_fusion.1.refs_8_), channel_id=1, source_target_pairs={{0,32},{1,33},{2,34},{3,35},{4,36},{5,37},{6,38},{7,39},{8,232},{9... | collective-permute-start | bytes 1007624 | tf_op jit(solution)/shard_map/ppermute | solution.py:46
  42.1 18.1 %collective-permute-start.13 = (bf16[2,656,128]{2,1,0:T(8,128)(2,1)S(1)}, bf16[2,656,128]{2,1,0:T(8,128)(2,1)S(1)}, u32[]{:S(2)}, u32[]{:S(2)}) collective-permute-start(bf16[2,656,128]{2,1,0:T(8,128)(2,1)S(1)} %pad_maximum_fusion.1.refs_8_), channel_id=1, source_target_pairs={{0,224},{1,225},{2,226},{3,227},{4,228},{5,229},{6,230},{7,231},{8... | collective-permute-start | bytes 1007624 | tf_op jit(solution)/shard_map/ppermute | solution.py:46
  45.3 18.2 %collective-permute-start.16 = (bf16[2,656,128]{2,1,0:T(8,128)(2,1)S(1)}, bf16[2,656,128]{2,1,0:T(8,128)(2,1)S(1)}, u32[]{:S(2)}, u32[]{:S(2)}) collective-permute-start(bf16[2,656,128]{2,1,0:T(8,128)(2,1)S(1)} %pad_maximum_fusion.1.refs_8_), channel_id=1, source_target_pairs={{0,8},{1,9},{2,10},{3,11},{4,12},{5,13},{6,14},{7,15},{8,0},{9,1},... | collective-permute-start | bytes 1007624 | tf_op jit(solution)/shard_map/ppermute | solution.py:46
  60.2 15.8 %collective-permute-start.10 = (bf16[2,656,128]{2,1,0:T(8,128)(2,1)S(1)}, bf16[2,656,128]{2,1,0:T(8,128)(2,1)}, u32[]{:S(2)}, u32[]{:S(2)}) collective-permute-start(bf16[2,656,128]{2,1,0:T(8,128)(2,1)S(1)} %collective-permute-done.9.refs_9_), channel_id=1, source_target_pairs={{0,32},{1,33},{2,34},{3,35},{4,36},{5,37},{6,38},{7,39},{8,232},{9... | collective-permute-start | bytes 1007624 | tf_op jit(solution)/shard_map/ppermute | solution.py:46
  60.2 16.5 %collective-permute-start.14 = (bf16[2,656,128]{2,1,0:T(8,128)(2,1)S(1)}, bf16[2,656,128]{2,1,0:T(8,128)(2,1)}, u32[]{:S(2)}, u32[]{:S(2)}) collective-permute-start(bf16[2,656,128]{2,1,0:T(8,128)(2,1)S(1)} %collective-permute-done.13.refs_15_), channel_id=1, source_target_pairs={{0,224},{1,225},{2,226},{3,227},{4,228},{5,229},{6,230},{7,231},{8... | collective-permute-start | bytes 1007624 | tf_op jit(solution)/shard_map/ppermute | solution.py:46
  63.4 14.4 %collective-permute-start.17 = (bf16[2,656,128]{2,1,0:T(8,128)(2,1)S(1)}, bf16[2,656,128]{2,1,0:T(8,128)(2,1)S(1)}, u32[]{:S(2)}, u32[]{:S(2)}) collective-permute-start(bf16[2,656,128]{2,1,0:T(8,128)(2,1)S(1)} %collective-permute-done.9.refs_9_), channel_id=1, source_target_pairs={{0,8},{1,9},{2,10},{3,11},{4,12},{5,13},{6,14},{7,15},{8,0},{9,1},... | collective-permute-start | bytes 1007624 | tf_op jit(solution)/shard_map/ppermute | solution.py:46
  63.4 19.0 %collective-permute-start.4 = (bf16[512,512]{1,0:T(8,128)(2,1)S(1)}, bf16[512,512]{1,0:T(8,128)(2,1)}, u32[]{:S(2)}, u32[]{:S(2)}) collective-permute-start(bf16[512,512]{1,0:T(8,128)(2,1)S(1)} %collective-permute-done.3.refs_4_), channel_id=1, source_target_pairs={{0,1},{1,2},{2,3},{3,0},{4,5},{5,6},{6,7},{7,4},{8,11},{9,8},{10,9... | collective-permute-start | bytes 1572872 | tf_op jit(solution)/shard_map/ppermute | solution.py:46
  64.3 31.7 %collective-permute-start.6 = (bf16[512,512]{1,0:T(8,128)(2,1)S(1)}, bf16[512,512]{1,0:T(8,128)(2,1)S(1)}, u32[]{:S(2)}, u32[]{:S(2)}) collective-permute-start(bf16[512,512]{1,0:T(8,128)(2,1)S(1)} %collective-permute-done.3.refs_4_), channel_id=1, source_target_pairs={{0,3},{1,0},{2,1},{3,2},{4,7},{5,4},{6,5},{7,6},{8,9},{9,10},{10,1... | collective-permute-start | bytes 1572872 | tf_op jit(solution)/shard_map/ppermute | solution.py:46
  76.0 4.5 %collective-permute-start.23 = (bf16[2,656,128]{2,1,0:T(8,128)(2,1)S(1)}, bf16[2,656,128]{2,1,0:T(8,128)(2,1)S(1)}, u32[]{:S(2)}, u32[]{:S(2)}) collective-permute-start(bf16[2,656,128]{2,1,0:T(8,128)(2,1)S(1)} %collective-permute-done.13.refs_15_), channel_id=1, source_target_pairs={{0,8},{1,9},{2,10},{3,11},{4,12},{5,13},{6,14},{7,15},{8,0},{9,1},... | collective-permute-start | bytes 1007624 | tf_op jit(solution)/shard_map/ppermute | solution.py:46
  76.7 16.8 %collective-permute-start.11 = (bf16[2,656,128]{2,1,0:T(8,128)(2,1)}, bf16[2,656,128]{2,1,0:T(8,128)(2,1)}, u32[]{:S(2)}, u32[]{:S(2)}) collective-permute-start(bf16[2,656,128]{2,1,0:T(8,128)(2,1)} %collective-permute-done.10.refs_10_), channel_id=1, source_target_pairs={{0,32},{1,33},{2,34},{3,35},{4,36},{5,37},{6,38},{7,39},{8,232},{9... | collective-permute-start | bytes 1007624 | tf_op jit(solution)/shard_map/ppermute | solution.py:46
  78.6 31.7 %collective-permute-start.1 = (bf16[512,512]{1,0:T(8,128)(2,1)S(1)}, bf16[512,512]{1,0:T(8,128)(2,1)}, u32[]{:S(2)}, u32[]{:S(2)}) collective-permute-start(bf16[512,512]{1,0:T(8,128)(2,1)S(1)} %collective-permute-done.refs_1_), channel_id=1, source_target_pairs={{0,1},{1,2},{2,3},{3,0},{4,5},{5,6},{6,7},{7,4},{8,11},{9,8},{10,9... | collective-permute-start | bytes 1572872 | tf_op jit(solution)/shard_map/ppermute | solution.py:46
  81.2 29.2 %collective-permute-start.15 = (bf16[2,656,128]{2,1,0:T(8,128)(2,1)}, bf16[2,656,128]{2,1,0:T(8,128)(2,1)}, u32[]{:S(2)}, u32[]{:S(2)}) collective-permute-start(bf16[2,656,128]{2,1,0:T(8,128)(2,1)} %collective-permute-done.14.refs_14_), channel_id=1, source_target_pairs={{0,224},{1,225},{2,226},{3,227},{4,228},{5,229},{6,230},{7,231},{8... | collective-permute-start | bytes 1007624 | tf_op jit(solution)/shard_map/ppermute | solution.py:46
  82.5 28.4 %collective-permute-start.18 = (bf16[2,656,128]{2,1,0:T(8,128)(2,1)}, bf16[2,656,128]{2,1,0:T(8,128)(2,1)}, u32[]{:S(2)}, u32[]{:S(2)}) collective-permute-start(bf16[2,656,128]{2,1,0:T(8,128)(2,1)} %collective-permute-done.10.refs_10_), channel_id=1, source_target_pairs={{0,8},{1,9},{2,10},{3,11},{4,12},{5,13},{6,14},{7,15},{8,0},{9,1},... | collective-permute-start | bytes 1007624 | tf_op jit(solution)/shard_map/ppermute | solution.py:46
  93.5 17.5 %collective-permute-start.12 = (bf16[2,656,128]{2,1,0:T(8,128)(2,1)}, bf16[2,656,128]{2,1,0:T(8,128)(2,1)}, u32[]{:S(2)}, u32[]{:S(2)}) collective-permute-start(bf16[2,656,128]{2,1,0:T(8,128)(2,1)} %collective-permute-done.11.refs_11_), channel_id=1, source_target_pairs={{0,32},{1,33},{2,34},{3,35},{4,36},{5,37},{6,38},{7,39},{8,232},{9... | collective-permute-start | bytes 1007624 | tf_op jit(solution)/shard_map/ppermute | solution.py:46
  96.0 9.0 %copy-start.2 = (bf16[512,512]{1,0:T(8,128)(2,1)}, bf16[512,512]{1,0:T(8,128)(2,1)S(1)}, u32[]{:S(2)}) copy-start(bf16[512,512]{1,0:T(8,128)(2,1)S(1)} %collective-permute-done.6.refs_7_) | copy-start | bytes 1572868
  96.0 24.5 %collective-permute-start.5 = (bf16[512,512]{1,0:T(8,128)(2,1)}, bf16[512,512]{1,0:T(8,128)(2,1)}, u32[]{:S(2)}, u32[]{:S(2)}) collective-permute-start(bf16[512,512]{1,0:T(8,128)(2,1)} %collective-permute-done.4.refs_5_), channel_id=1, source_target_pairs={{0,1},{1,2},{2,3},{3,0},{4,5},{5,6},{6,7},{7,4},{8,11},{9,8},{10,9... | collective-permute-start | bytes 1572872 | tf_op jit(solution)/shard_map/ppermute | solution.py:46
  105.0 15.5 %all-to-all-start = ((bf16[64,8,512]{2,0,1:T(8,128)(2,1)}), bf16[64,8,512]{2,0,1:T(8,128)(2,1)S(1)}, u32[]{:S(2)}, u32[]{:S(2)}) async-start(bf16[64,8,512]{2,0,1:T(8,128)(2,1)} %bitcast.38), calls=%async_computation | async-start | bytes 1048576 | tf_op jit(solution)/shard_map/all_to_all | solution.py:304
  110.2 10.2 %collective-permute-start.22 = (bf16[2,656,128]{2,1,0:T(8,128)(2,1)}, bf16[2,656,128]{2,1,0:T(8,128)(2,1)}, u32[]{:S(2)}, u32[]{:S(2)}) collective-permute-start(bf16[2,656,128]{2,1,0:T(8,128)(2,1)} %collective-permute-done.14.refs_14_), channel_id=1, source_target_pairs={{0,8},{1,9},{2,10},{3,11},{4,12},{5,13},{6,14},{7,15},{8,0},{9,1},... | collective-permute-start | bytes 1007624 | tf_op jit(solution)/shard_map/ppermute | solution.py:46
  110.4 10.1 %collective-permute-start.19 = (bf16[2,656,128]{2,1,0:T(8,128)(2,1)}, bf16[2,656,128]{2,1,0:T(8,128)(2,1)}, u32[]{:S(2)}, u32[]{:S(2)}) collective-permute-start(bf16[2,656,128]{2,1,0:T(8,128)(2,1)} %collective-permute-done.11.refs_11_), channel_id=1, source_target_pairs={{0,8},{1,9},{2,10},{3,11},{4,12},{5,13},{6,14},{7,15},{8,0},{9,1},... | collective-permute-start | bytes 1007624 | tf_op jit(solution)/shard_map/ppermute | solution.py:46
  110.8 9.6 %collective-permute-start.21 = (bf16[2,656,128]{2,1,0:T(8,128)(2,1)}, bf16[2,656,128]{2,1,0:T(8,128)(2,1)}, u32[]{:S(2)}, u32[]{:S(2)}) collective-permute-start(bf16[2,656,128]{2,1,0:T(8,128)(2,1)} %collective-permute-done.15.refs_13_), channel_id=1, source_target_pairs={{0,8},{1,9},{2,10},{3,11},{4,12},{5,13},{6,14},{7,15},{8,0},{9,1},... | collective-permute-start | bytes 1007624 | tf_op jit(solution)/shard_map/ppermute | solution.py:46
  111.0 9.5 %collective-permute-start.20 = (bf16[2,656,128]{2,1,0:T(8,128)(2,1)}, bf16[2,656,128]{2,1,0:T(8,128)(2,1)}, u32[]{:S(2)}, u32[]{:S(2)}) collective-permute-start(bf16[2,656,128]{2,1,0:T(8,128)(2,1)} %collective-permute-done.12.refs_12_), channel_id=1, source_target_pairs={{0,8},{1,9},{2,10},{3,11},{4,12},{5,13},{6,14},{7,15},{8,0},{9,1},... | collective-permute-start | bytes 1007624 | tf_op jit(solution)/shard_map/ppermute | solution.py:46
  120.5 1.0 copy-start.3
  125.4 23.2 %copy-start.21 = (bf16[4096]{0:T(1024)(128)(2,1)S(1)}, bf16[4096]{0:T(1024)(128)(2,1)}, u32[]{:S(2)}) copy-start(bf16[4096]{0:T(1024)(128)(2,1)} %param.19) | copy-start | bytes 24580
  125.4 23.2 %copy-start.20 = (f32[3,7,512]{2,1,0:T(8,128)S(1)}, f32[3,7,512]{2,1,0:T(8,128)}, u32[]{:S(2)}) copy-start(f32[3,7,512]{2,1,0:T(8,128)} %param.21) | copy-start | bytes 129028
  136.7 10.8 %collective-permute-start.27 = (bf16[512,512]{1,0:T(8,128)(2,1)S(1)}, bf16[512,512]{1,0:T(8,128)(2,1)S(1)}, u32[]{:S(2)}, u32[]{:S(2)}) collective-permute-start(bf16[512,512]{1,0:T(8,128)(2,1)S(1)} %m1.1.refs_0_), channel_id=1, source_target_pairs={{0,4},{1,5},{2,6},{3,7},{4,0},{5,1},{6,2},{7,3},{8,12},{9,13},{10,... | collective-permute-start | bytes 1572872 | tf_op jit(solution)/shard_map/ppermute | solution.py:46
  137.4 16.9 %collective-permute-start.24 = (bf16[512,512]{1,0:T(8,128)(2,1)S(1)}, bf16[512,512]{1,0:T(8,128)(2,1)S(1)}, u32[]{:S(2)}, u32[]{:S(2)}) collective-permute-start(bf16[512,512]{1,0:T(8,128)(2,1)S(1)} %m1.1.refs_0_), channel_id=1, source_target_pairs={{0,1},{1,2},{2,3},{3,0},{4,5},{5,6},{6,7},{7,4},{8,11},{9,8},{10,9... | collective-permute-start | bytes 1572872 | tf_op jit(solution)/shard_map/ppermute | solution.py:46
  147.5 16.5 %collective-permute-start.28 = (bf16[512,512]{1,0:T(8,128)(2,1)S(1)}, bf16[512,512]{1,0:T(8,128)(2,1)S(1)}, u32[]{:S(2)}, u32[]{:S(2)}) collective-permute-start(bf16[512,512]{1,0:T(8,128)(2,1)S(1)} %collective-permute-done.27.refs_4_), channel_id=1, source_target_pairs={{0,1},{1,2},{2,3},{3,0},{4,5},{5,6},{6,7},{7,4},{8,11},{9,8},{10,9... | collective-permute-start | bytes 1572872 | tf_op jit(solution)/shard_map/ppermute | solution.py:46
  148.7 15.4 %collective-permute-start.26 = (bf16[512,512]{1,0:T(8,128)(2,1)S(1)}, bf16[512,512]{1,0:T(8,128)(2,1)S(1)}, u32[]{:S(2)}, u32[]{:S(2)}) collective-permute-start(bf16[512,512]{1,0:T(8,128)(2,1)S(1)} %m1.1.refs_0_), channel_id=1, source_target_pairs={{0,3},{1,0},{2,1},{3,2},{4,7},{5,4},{6,5},{7,6},{8,9},{9,10},{10,1... | collective-permute-start | bytes 1572872 | tf_op jit(solution)/shard_map/ppermute | solution.py:46
  152.3 22.8 %collective-permute-start.30 = (bf16[512,512]{1,0:T(8,128)(2,1)S(1)}, bf16[512,512]{1,0:T(8,128)(2,1)S(1)}, u32[]{:S(2)}, u32[]{:S(2)}) collective-permute-start(bf16[512,512]{1,0:T(8,128)(2,1)S(1)} %collective-permute-done.27.refs_4_), channel_id=1, source_target_pairs={{0,3},{1,0},{2,1},{3,2},{4,7},{5,4},{6,5},{7,6},{8,9},{9,10},{10,1... | collective-permute-start | bytes 1572872 | tf_op jit(solution)/shard_map/ppermute | solution.py:46
  154.3 20.5 %collective-permute-start.25 = (bf16[512,512]{1,0:T(8,128)(2,1)S(1)}, bf16[512,512]{1,0:T(8,128)(2,1)S(1)}, u32[]{:S(2)}, u32[]{:S(2)}) collective-permute-start(bf16[512,512]{1,0:T(8,128)(2,1)S(1)} %collective-permute-done.24.refs_1_), channel_id=1, source_target_pairs={{0,1},{1,2},{2,3},{3,0},{4,5},{5,6},{6,7},{7,4},{8,11},{9,8},{10,9... | collective-permute-start | bytes 1572872 | tf_op jit(solution)/shard_map/ppermute | solution.py:46
  164.0 16.4 %collective-permute-start.29 = (bf16[512,512]{1,0:T(8,128)(2,1)S(1)}, bf16[512,512]{1,0:T(8,128)(2,1)S(1)}, u32[]{:S(2)}, u32[]{:S(2)}) collective-permute-start(bf16[512,512]{1,0:T(8,128)(2,1)S(1)} %collective-permute-done.28.refs_5_), channel_id=1, source_target_pairs={{0,1},{1,2},{2,3},{3,0},{4,5},{5,6},{6,7},{7,4},{8,11},{9,8},{10,9... | collective-permute-start | bytes 1572872 | tf_op jit(solution)/shard_map/ppermute | solution.py:46
  180.4 1.0 copy-start.5
  199.0 7.3 %collective-permute-start.31 = (bf16[3,6,512]{2,1,0:T(8,128)(2,1)S(1)}, bf16[3,6,512]{2,1,0:T(8,128)(2,1)S(1)}, u32[]{:S(2)}, u32[]{:S(2)}) collective-permute-start(bf16[3,6,512]{2,1,0:T(8,128)(2,1)S(1)} %slice.59), channel_id=1, source_target_pairs={{0,8},{8,16},{16,24},{24,32},{32,40},{40,48},{48,56},{56,64},{64,7... | collective-permute-start | bytes 55304 | tf_op jit(solution)/shard_map/ppermute | solution.py:257
  213.6 8.7 %copy-start.14 = (f32[128,512]{1,0:T(8,128)S(1)}, f32[128,512]{1,0:T(8,128)}, u32[]{:S(2)}) copy-start(f32[128,512]{1,0:T(8,128)} %taps.1) | copy-start | bytes 786436
  213.6 8.7 %copy-start.15 = (f32[512]{0:T(512)S(1)}, f32[512]{0:T(512)}, u32[]{:S(2)}) copy-start(f32[512]{0:T(512)} %param.23) | copy-start | bytes 6148
  213.7 8.7 %copy-start.16 = (bf16[256,256]{1,0:T(8,128)(2,1)S(1)}, bf16[256,256]{1,0:T(8,128)(2,1)}, u32[]{:S(2)}) copy-start(bf16[256,256]{1,0:T(8,128)(2,1)} %constant.132.clone.f_hi) | copy-start | bytes 393220
  213.7 8.7 %copy-start.17 = (bf16[256,256]{1,0:T(8,128)(2,1)S(1)}, bf16[256,256]{1,0:T(8,128)(2,1)}, u32[]{:S(2)}) copy-start(bf16[256,256]{1,0:T(8,128)(2,1)} %constant.133.clone.f_lo) | copy-start | bytes 393220
  213.7 8.7 %copy-start.18 = (bf16[128,256]{1,0:T(8,128)(2,1)S(1)}, bf16[128,256]{1,0:T(8,128)(2,1)}, u32[]{:S(2)}) copy-start(bf16[128,256]{1,0:T(8,128)(2,1)} %constant.134.clone.g_hi) | copy-start | bytes 196612
  213.7 8.7 %copy-start.19 = (bf16[128,256]{1,0:T(8,128)(2,1)S(1)}, bf16[128,256]{1,0:T(8,128)(2,1)}, u32[]{:S(2)}) copy-start(bf16[128,256]{1,0:T(8,128)(2,1)} %constant.135.clone.g_lo) | copy-start | bytes 196612
  214.0 8.4 %collective-permute-start.32 = (bf16[128,512]{1,0:T(8,128)(2,1)S(1)}, bf16[128,512]{1,0:T(8,128)(2,1)S(1)}, u32[]{:S(2)}, u32[]{:S(2)}) collective-permute-start(bf16[128,512]{1,0:T(8,128)(2,1)S(1)} %slice_bitcast_fusion.1), channel_id=1, source_target_pairs={{0,8},{8,16},{16,24},{24,32},{32,40},{40,48},{48,56},{56,64},{64,7... | collective-permute-start | bytes 393224 | tf_op jit(solution)/shard_map/ppermute | solution.py:257
  (10 other events, 8.5 us)
Sparse Core Ops, SparseCore 0:
  9.9 111.5 all-gather.2
